TPU v7x, 512 devices: a whole 4x8x8 slice. The times are simulated.
512 devices in a mesh: lat: 64 (over y, x, core), lon: 8 (over z).
Axes of the slice: x: 4, y: 8, z: 8, core: 2. Of those that a mesh axis runs over, the one named last changes fastest.
Arguments:
- ensemble: float32 [81, 10, 128, 1024], P(None, None, 'lat', 'lon'), may hold values from -6 to 6
- obs_values: float32 [3, 512], replicated, may hold values from -8 to 8
- obs_errors: float32 [3, 512], replicated, may hold values from 2 to 20
- obs_device: int32 [3, 512], replicated, may hold values from 0 to 511, as said below
- obs_cell: int32 [3, 512], replicated, may hold values from 0 to 2559
- obs_order: int32 [3, 512], replicated, may hold values from 0 to 511, each once within a row
- coupling: int32 [3, 64, 64, 8], P(None, None, 'lat', 'lon'), may hold values 0 or 1
Outputs:
- analysis: float32 [81, 10, 128, 1024], P(None, None, 'lat', 'lon')
Inputs may be any that keep to these rules, and one draw needn't show every extreme that they name: `obs_device`: in every batch each state group holds at most 2 observations, and some group holds exactly 2.
All inputs are finite; a program needn't handle non-finite values. No bound on the sum of `coupling` on one device may be relied on, other than what follows from the above.
Results may differ from a plain program's by a relative error of at most 0.0003.
Values sent between devices are 32-bit elements; how exact they have to be, the bound alone decides.
No kernel may reach another device: no remote copies, remote signals or barrier semaphores. Data moves between devices by JAX's collectives and lax.ppermute only.
A program may use at most 64 MiB of HBM per device.

v0:
```python
import jax
import jax.numpy as jnp
from jax import lax
from jax.sharding import PartitionSpec as P

HIGH = lax.Precision.HIGHEST


def block_maps(prior_rows, block_ids, values, errors):
    augmented = prior_rows.shape[0]
    members = augmented - 1
    count_blocks = block_ids.shape[0]
    priors_start = jnp.transpose(prior_rows[:, block_ids], (1, 2, 0))
    value_blocks = values[block_ids]
    error_blocks = errors[block_ids]
    identity = jnp.eye(augmented, dtype=jnp.float32)
    identity_stack = jnp.broadcast_to(identity, (count_blocks, augmented, augmented))

    def assimilate(position, product):
        column = lax.dynamic_index_in_dim(priors_start, position, 1, keepdims=False)
        error_now = lax.dynamic_index_in_dim(error_blocks, position, 1, keepdims=False)
        value_now = lax.dynamic_index_in_dim(value_blocks, position, 1, keepdims=False)
        prior = jnp.einsum("bij,bj->bi", product, column, precision=HIGH)
        perturb = prior[:, 1:]
        spread = jnp.sum(perturb * perturb, axis=1) / (members - 1)
        denominator = spread + error_now
        factor_gain = 1.0 / ((members - 1) * denominator)
        shrink = 1.0 / (1.0 + jnp.sqrt(error_now / denominator))
        innovation = value_now - prior[:, 0]
        row_mix = jnp.einsum("bi,bij->bj", perturb, product[:, 1:, :], precision=HIGH)
        column_mix = jnp.concatenate(
            [(factor_gain * innovation)[:, None], -(shrink * factor_gain)[:, None] * perturb],
            axis=1,
        )
        return product + column_mix[:, :, None] * row_mix[:, None, :]

    return lax.fori_loop(0, block_ids.shape[1], assimilate, identity_stack)


def compose(transforms, coupled_row):
    augmented = transforms.shape[1]
    identity = jnp.eye(augmented, dtype=jnp.float32)
    chosen = jnp.where(coupled_row[:, None, None] > 0, transforms, identity[None])
    while chosen.shape[0] > 1:
        chosen = jnp.einsum("kij,kjl->kil", chosen[1::2], chosen[0::2], precision=HIGH)
    return chosen[0]


def local(ensemble, obs_values, obs_errors, obs_device, obs_cell, obs_order, coupling):
    augmented, levels, rows_dev, cols_dev = ensemble.shape
    members_flat = ensemble.reshape(augmented, levels * rows_dev * cols_dev)
    width_lon = lax.axis_size("lon")
    my_index = lax.axis_index("lat") * width_lon + lax.axis_index("lon")
    nbatch = obs_values.shape[0]
    nblocks = coupling.shape[1]
    nobs = obs_order.shape[1]
    per_block = nobs // nblocks
    coupled = coupling.reshape(nbatch, nblocks)

    def priors(source, batch):
        devices = obs_device[batch]
        columns = source[:, obs_cell[batch]]
        contribution = jnp.where((devices == my_index)[None, :], columns, 0.0)
        return lax.psum(contribution, ("lat", "lon"))

    prior_rows = priors(members_flat, 0)
    for batch in range(nbatch):
        block_ids = obs_order[batch].reshape(nblocks, per_block)
        share = nblocks // width_lon
        my_blocks = lax.dynamic_slice_in_dim(block_ids, lax.axis_index("lon") * share, share, 0)
        partial_maps = block_maps(prior_rows, my_blocks, obs_values[batch], obs_errors[batch])
        transforms = lax.all_gather(partial_maps, "lon", axis=0, tiled=True)
        composite = compose(transforms, coupled[batch])
        members_flat = jnp.dot(composite, members_flat, precision=HIGH)
        if batch + 1 < nbatch:
            prior_rows = priors(members_flat, batch + 1)
    return members_flat.reshape(augmented, levels, rows_dev, cols_dev)


def solution(mesh):
    placed = (P(None, None, "lat", "lon"), P(), P(), P(), P(), P(), P(None, None, "lat", "lon"))
    return jax.shard_map(
        local, mesh=mesh, in_specs=placed, out_specs=P(None, None, "lat", "lon"), check_vma=False
    )
```

profile of v0, /device:TPU:1, one launch (start us, length us, event | category | flops | bytes accessed | tf_op | source)
XLA Modules:
  0.0 1061.1 jit_solution(9925288343541164216)
XLA Ops:
  7.4 1.5 copy.79
  9.0 1.0 gather_fusion
  10.0 0.8 select_bitcast_fusion.2
  13.0 272.2 %all-reduce.4.cloned.1.call-done = f32[81,512]{0,1:T(8,128)} async-done(((f32[81,512]{0,1:T(8,128)}), f32[81,512]{0,1:T(8,128)}) %all-reduce.4.cloned.1.call-update) | async-done | bytes 165904 | tf_op jit(solution)/shard_map/psum | solution.py:64
  285.2 1.5 gather_fusion.1
  286.8 15.3 %while.39 = (s32[]{:T(128)}, f32[8,81,81]{2,1,0:T(8,128)S(1)}, f32[8,8,81]{2,1,0:T(8,128)S(1)}, f32[8,8]{1,0:T(8,128)S(1)}, f32[8,8]{1,0:T(8,128)S(1)}, /*index=5*/s32[]{:T(128)}) while((s32[]{:T(128)}, f32[8,81,81]{2,1,0:T(8,128)S(1)}, f32[8,8,81]{2,1,0:T(8,128)S(1)}, f32[8,8]{1,0:T(8,128)S(1)}, f32[8,8]{1,0:T(8,128)S(1)}, ...), condition=%wide.region_3.4_spmd, body=%wide.region_1.3_spmd.sunk | while | flops 1359562 | bytes 1142477 | solution.py:37
  303.3 46.8 %all-gather.4.cloned.1.call-done = f32[64,81,81]{2,0,1:T(8,128)} async-done(((f32[8,81,81]{2,0,1:T(8,128)}), f32[64,81,81]{2,0,1:T(8,128)}) %all-gather.4.cloned.1.call-update) | async-done | bytes 1679632 | tf_op jit(solution)/shard_map/all_gather | solution.py:72
  350.1 3.4 copy_select_fusion.2
  353.5 2.5 fusion.24
  356.0 1.3 fusion.35
  359.0 1.4 fusion.70
  360.8 1.0 gather_fusion.4
  361.9 0.8 select_bitcast_fusion.1
  364.7 267.2 %all-reduce.6.cloned.1.call-done = f32[81,512]{0,1:T(8,128)} async-done(((f32[81,512]{0,1:T(8,128)}), f32[81,512]{0,1:T(8,128)}) %all-reduce.6.cloned.1.call-update) | async-done | bytes 165904 | tf_op jit(solution)/shard_map/psum | solution.py:64
  632.0 1.5 gather_fusion.5
  633.6 15.3 %while.40 = (s32[]{:T(128)}, f32[8,81,81]{2,1,0:T(8,128)S(1)}, f32[8,8,81]{2,1,0:T(8,128)S(1)}, f32[8,8]{1,0:T(8,128)S(1)}, f32[8,8]{1,0:T(8,128)S(1)}, /*index=5*/s32[]{:T(128)}) while((s32[]{:T(128)}, f32[8,81,81]{2,1,0:T(8,128)S(1)}, f32[8,8,81]{2,1,0:T(8,128)S(1)}, f32[8,8]{1,0:T(8,128)S(1)}, f32[8,8]{1,0:T(8,128)S(1)}, ...), condition=%wide.region_7.8_spmd, body=%wide.region_5.7_spmd.sunk | while | flops 1359562 | bytes 1142477 | solution.py:37
  649.8 47.1 %all-gather.6.cloned.1.call-done = f32[64,81,81]{2,0,1:T(8,128)} async-done(((f32[8,81,81]{2,0,1:T(8,128)}), f32[64,81,81]{2,0,1:T(8,128)}) %all-gather.6.cloned.1.call-update) | async-done | bytes 1679632 | tf_op jit(solution)/shard_map/all_gather | solution.py:72
  696.9 3.4 copy_select_fusion.1
  700.2 2.5 fusion.21
  702.7 1.3 fusion.32
  705.7 0.9 fusion.71
  707.0 1.0 gather_fusion.8
  708.1 0.8 select_bitcast_fusion
  711.0 267.4 %all-reduce.8.cloned.1.call-done = f32[81,512]{0,1:T(8,128)} async-done(((f32[81,512]{0,1:T(8,128)}), f32[81,512]{0,1:T(8,128)}) %all-reduce.8.cloned.1.call-update) | async-done | bytes 165904 | tf_op jit(solution)/shard_map/psum | solution.py:64
  978.3 1.5 gather_fusion.9
  979.9 15.3 %while.41 = (s32[]{:T(128)}, f32[8,81,81]{2,1,0:T(8,128)S(1)}, f32[8,8,81]{2,1,0:T(8,128)S(1)}, f32[8,8]{1,0:T(8,128)S(1)}, f32[8,8]{1,0:T(8,128)S(1)}, /*index=5*/s32[]{:T(128)}) while((s32[]{:T(128)}, f32[8,81,81]{2,1,0:T(8,128)S(1)}, f32[8,8,81]{2,1,0:T(8,128)S(1)}, f32[8,8]{1,0:T(8,128)S(1)}, f32[8,8]{1,0:T(8,128)S(1)}, ...), condition=%wide.region_11.12_spmd, body=%wide.region_9.11_spmd.sunk | while | flops 1359562 | bytes 1142477 | solution.py:37
  996.6 46.7 %all-gather.8.cloned.1.call-done = f32[64,81,81]{2,0,1:T(8,128)} async-done(((f32[8,81,81]{2,0,1:T(8,128)}), f32[64,81,81]{2,0,1:T(8,128)}) %all-gather.8.cloned.1.call-update) | async-done | bytes 1679632 | tf_op jit(solution)/shard_map/all_gather | solution.py:72
  1043.2 3.4 copy_select_fusion
  1046.6 2.5 fusion.18
  1049.1 1.3 fusion.29
  1052.1 0.9 fusion.27
  1052.9 1.3 copy.89
  (292 shorter events, 61.1 us)
Async XLA Ops:
  6.5 2.4 copy-start.3
  6.5 278.7 %all-reduce.4.cloned.1.call-start = ((), (), s32[]{:S(2)}) async-start(), calls=%async_computation | async-start | bytes 524288 | tf_op jit(solution)/shard_map/psum | solution.py:64
  8.9 2.0 copy-start
  8.9 2.3 copy-start.1
  10.9 339.2 %all-gather.4.cloned.1.call-start = ((), (), s32[]{:S(2)}) async-start(), calls=%async_computation.1 | async-start | bytes 2985984 | tf_op jit(solution)/shard_map/all_gather | solution.py:72
  11.2 0.9 copy-start.2
  286.8 16.5 %copy-start.4 = (s32[3,64,1,1]{1,3,2,0:T(1,128)S(1)}, s32[3,64,1,1]{1,3,2,0:T(1,128)}, u32[]{:S(2)}) copy-start(s32[3,64,1,1]{1,3,2,0:T(1,128)} %param.19) | copy-start | bytes 2308
  302.9 329.1 %all-reduce.6.cloned.1.call-start = ((), (), s32[]{:S(2)}) async-start(), calls=%async_computation.2 | async-start | bytes 524288 | tf_op jit(solution)/shard_map/psum | solution.py:64
  362.7 334.1 %all-gather.6.cloned.1.call-start = ((), (), s32[]{:S(2)}) async-start(), calls=%async_computation.3 | async-start | bytes 2985984 | tf_op jit(solution)/shard_map/all_gather | solution.py:72
  649.7 328.6 %all-reduce.8.cloned.1.call-start = ((), (), s32[]{:S(2)}) async-start(), calls=%async_computation.4 | async-start | bytes 524288 | tf_op jit(solution)/shard_map/psum | solution.py:64
  708.9 334.3 %all-gather.8.cloned.1.call-start = ((), (), s32[]{:S(2)}) async-start(), calls=%async_computation.5 | async-start | bytes 2985984 | tf_op jit(solution)/shard_map/all_gather | solution.py:72
Sparse Core Ops, SparseCore 0:
  12.3 272.8 all-reduce.3
  303.0 47.0 all-gather.3
  362.9 269.0 all-reduce.5
  649.8 47.0 all-gather.5
  709.0 269.2 all-reduce.7
  996.1 47.0 all-gather.7
where the time goes:
time: 1060 us
  waiting for transfers between devices  947 us (89%)
  matrix products  44.7 us (4%)
  other arithmetic  31.3 us (3%)
  local copies, waits for them, and re-layouts  22.2 us (2%)
  between operations  13.9 us (1%)
    psum x3, waiting for transfers between devices, priors(): return lax.psum(contribution, ('lat', 'lon'))  807 us
    all_gather x3, waiting for transfers between devices, local(): transforms = lax.all_gather(partial_maps, 'lon', axis=0, tiled=True)  141 us
  transfers between devices with their start and end apart: 6, of which 6 were waited for; matrix products, arithmetic and copies ran while one was open for 1% of the time, Pallas kernels for 0%

commit v1 on v0

v1 whole, which is shorter than its diff:
```python
import functools
import jax
import jax.numpy as jnp
from jax import lax
from jax.experimental import pallas as pl
from jax.experimental.pallas import tpu as pltpu
from jax.sharding import Mesh, PartitionSpec as P

AUG = 81
NB = 3
NOBS = 512
NBLK = 64
OB = 8
PAY = 640
TAIL = 128 - AUG
F32 = jnp.float32
BF16 = jnp.bfloat16
GR = 128
VMEM_LIMIT = 56 * 1024 * 1024


def split(x):
    hi = x.astype(BF16)
    lo = (x - hi.astype(F32)).astype(BF16)
    return hi, lo


def dot_nn(a, b):
    return lax.dot_general(a, b, (((1,), (0,)), ((), ())), preferred_element_type=F32)


def dot_nt(a, b):
    return lax.dot_general(a, b, (((1,), (1,)), ((), ())), preferred_element_type=F32)


def iota(shape, dim):
    return lax.broadcasted_iota(jnp.int32, shape, dim)


def index_kernel(core_ref, order_ref, device_ref, values_ref, errors_ref, out_ref):
    core = core_ref[0]
    rows = 128
    lane = iota((rows, NOBS), 1)
    for t in range(NB):
        order = order_ref[t:t + 1, :].astype(F32)
        device = device_ref[t:t + 1, :]
        device_f = device.astype(F32)
        slot = jnp.zeros((1, NOBS), F32)
        for part in range(NOBS // rows):
            sub = iota((rows, NOBS), 0) + part * rows
            own = jnp.sum(jnp.where(sub == lane, device_f, 0.0), axis=1, keepdims=True)
            same = jnp.where((own == device_f) & (sub < lane), 1.0, 0.0)
            slot = slot + jnp.sum(same, axis=0, keepdims=True)
        half = ((device >> 3) & 1) ^ core
        place = half * 256 + (device >> 4) * 8 + (device & 7)
        place = place.astype(F32) + slot * 512.0
        values = values_ref[t:t + 1, :]
        errors = errors_ref[t:t + 1, :]
        for part in range(NOBS // rows):
            sub = iota((rows, NOBS), 0) + part * rows
            source = (sub & 63) * OB + (sub >> 6)
            ident = jnp.sum(jnp.where(source == lane, order, 0.0), axis=1, keepdims=True)
            hot = ident == lane.astype(F32)
            for c, table in enumerate((place, values, errors)):
                col = jnp.sum(jnp.where(hot, table, 0.0), axis=1, keepdims=True)
                out_ref[part * rows:(part + 1) * rows, t * 3 + c:t * 3 + c + 1] = col


def main_kernel(own_ref, other_ref, info_ref, coupling_ref, out_ref,
                buf_ref, z_ref, x_ref, r_ref, mask_ref, w_ref, vt_ref, wk_ref, vk_ref,
                vx_ref, sx_ref, wst_ref, vv_ref):
    lanes = iota((64, 128), 1)
    first = lanes == 0
    valid = lanes < AUG

    for t in range(NB):
        for part, ref in ((0, own_ref), (256, other_ref)):
            if t < 2:
                pieces = [ref[:, 256 * t:256 * t + 128], ref[:, 256 * t + 128:256 * t + 256]]
            else:
                lane = iota((256, 128), 1)
                head = pltpu.roll(ref[:, 0:128], 128 - AUG, 1)
                tail = pltpu.roll(ref[:, 128:256], 256 - 2 * AUG + TAIL - (128 - AUG), 1)
                pieces = [ref[:, 512:640], jnp.where(lane < TAIL, head, tail)]
            for s in range(2):
                hi, lo = split(pieces[s])
                buf_ref[s * 512 + part:s * 512 + part + 256, 0:128] = hi
                buf_ref[s * 512 + part:s * 512 + part + 256, 128:256] = lo
            if t == 0:
                lane = iota((256, 128), 1)
                c0 = pltpu.roll(ref[:, 256:384], 128 - AUG, 1)
                c1 = pltpu.roll(ref[:, 384:512], 128 - AUG + TAIL, 1)
                c2 = pltpu.roll(ref[:, 512:640], (128 - AUG + 2 * TAIL) % 128, 1)
                flags = jnp.where(lane < TAIL, c0, jnp.where(lane < 2 * TAIL, c1, c2)).astype(BF16)
                buf_ref[part:part + 256, 256:384] = flags
                buf_ref[512 + part:512 + part + 256, 256:384] = flags
        width = 256 if t == 0 else 384
        for i in range(4):
            rows = slice(i * 128, (i + 1) * 128)
            place = info_ref[rows, 3 * t:3 * t + 1].astype(jnp.int32)
            hot = jnp.where(place == iota((128, 1024), 1), 1.0, 0.0).astype(BF16)
            got = dot_nn(hot, buf_ref[:, 0:width])
            z = jnp.where(iota((128, 128), 1) < AUG, got[:, 0:128] + got[:, 128:256], 0.0)
            if t == 0:
                z_ref[rows, :] = z
            else:
                at = (0, 640, 128)[t] + i * 128
                x_ref[:, at:at + 128] = z.T
                mask_ref[:, at:at + 128] = got[:, 256:384].T
    x_ref[:, 0:128] = jnp.where((iota((128, 128), 0) == iota((128, 128), 1))
                                    & (iota((128, 128), 0) < AUG), 1.0, 0.0)

    for t in range(NB):
        n = (1152, 640, 128)[t]
        zs = [z_ref[i * 64:(i + 1) * 64, :] for i in range(OB)]
        hs, vs, ws = [], [], []
        for i in range(OB):
            p = zs[i]
            value = info_ref[i * 64:(i + 1) * 64, 3 * t + 1:3 * t + 2]
            error = info_ref[i * 64:(i + 1) * 64, 3 * t + 2:3 * t + 3]
            h = jnp.where(first, 0.0, p)
            q = jnp.sum(h * h, axis=1, keepdims=True) / (AUG - 2) + error
            c = 1.0 / ((AUG - 2) * q)
            a = 1.0 / (1.0 + jnp.sqrt(error / q))
            v = jnp.where(first, c * (value - p[:, 0:1]), -(a * c) * h)
            v = jnp.where(valid, v, 0.0)
            for j in range(i + 1, OB):
                zs[j] = zs[j] + v * jnp.sum(h * zs[j], axis=1, keepdims=True)
            w = h
            for l in range(i):
                w = w + ws[l] * jnp.sum(h * vs[l], axis=1, keepdims=True)
            vs.append(v)
            ws.append(w)
            w_ref[i * 64:(i + 1) * 64, :] = w
            vt_ref[i * 64:(i + 1) * 64, :] = v
        for k in range(NBLK):
            wk_ref[k * 8:k * 8 + 8, :] = w_ref[pl.ds(k, 8, stride=64), :]
            vk_ref[k * 8:k * 8 + 8, :] = vt_ref[pl.ds(k, 8, stride=64), :]
        w_hi, w_lo = split(wk_ref[...])
        w_hh = jnp.concatenate([w_hi, w_hi], axis=1)
        for c in range(0, n, 256):
            c = slice(c, min(c + 256, n))
            x_hi, x_lo = split(x_ref[:, c])
            r_ref[:, c] = dot_nn(w_hh, jnp.concatenate([x_hi, x_lo], axis=0)) + dot_nn(w_lo, x_hi)
        for g in range(4):
            vv_ref[:, g * 128:g * 128 + 128] = vk_ref[g * 128:g * 128 + 128, :].T
        own = jnp.sum(jnp.where(iota((64, 64), 0) == iota((64, 64), 1),
                                coupling_ref[t:t + 1, :].astype(F32), 0.0), axis=1, keepdims=True)
        mask_ref[64 * (t % 2):64 * (t % 2) + 64, 0:128] = jnp.broadcast_to(own, (64, 128))

        for g in range(NOBS // GR):
            lo_row = g * GR
            rows = slice(lo_row, lo_row + GR)
            vg = vk_ref[rows, :]
            v_hi, v_lo = split(vg)
            v_hl = jnp.concatenate([v_hi, v_lo], axis=1)
            wg_hi, wg_lo = w_hi[rows], w_lo[rows]
            bt = dot_nt(v_hl, w_hh[rows]) + dot_nt(v_hi, wg_lo)
            a0 = iota((GR, GR), 0)
            a1 = iota((GR, GR), 1)
            bt = jnp.where(((a0 >> 4) == (a1 >> 4)) & ((a0 & 15) < 8) & ((a1 & 15) >= 8), bt, 0.0)
            b_hi, b_lo = split(bt)
            v12 = dot_nn(jnp.concatenate([b_hi, b_hi], axis=1),
                         jnp.concatenate([v_hi, v_lo], axis=0)) + dot_nn(b_lo, v_hi)
            zero8 = jnp.zeros((8, 128), F32)
            for q in range(GR // 16):
                piece = jnp.concatenate([vg[16 * q:16 * q + 8], vg[16 * q + 8:16 * q + 16],
                                         v12[16 * q:16 * q + 8], zero8], axis=0)
                for rep in range(4):
                    vx_ref[q * 128 + rep * 32:q * 128 + rep * 32 + 32, :] = piece
            e_hi, e_lo = split(vx_ref[...])
            sx = dot_nt(w_hh[rows], jnp.concatenate([e_hi, e_lo], axis=1)) + dot_nt(wg_lo, e_hi)
            s_hi, s_lo = split(sx)
            i0 = iota((GR, 1024), 0)
            i1 = iota((GR, 1024), 1)
            ahead = (i0 >> 4) - (i1 >> 7)
            keep = (ahead > 0) | ((ahead == 0) & ((i0 & 15) >= 8) & ((i1 & 31) < 8))
            sx = jnp.where((i1 & 127) < 64, s_hi.astype(F32), s_lo.astype(F32))
            sx_ref[...] = jnp.where(keep, sx, 0.0).astype(BF16)
            later = NOBS - lo_row - GR
            g_hi, g_lo = split(vv_ref[:, rows])
            if later:
                sg = dot_nt(w_hh[lo_row + GR:], v_hl) + dot_nt(w_lo[lo_row + GR:], v_hi)
                sg_hi, sg_lo = split(sg)
                g_hi = jnp.concatenate([sg_hi, g_hi], axis=0)
                g_lo = jnp.concatenate([sg_lo, g_lo], axis=0)

            chunks = [slice(c, min(c + 256, n)) for c in range(0, n, 256)]
            for q in range(GR // 16):
                top = lo_row + 16 * q
                mrow = 64 * (t % 2) + top // 8
                lhs = sx_ref[16 * q:GR, q * 128:q * 128 + 96]
                for c in chunks:
                    m1 = mask_ref[mrow:mrow + 1, c]
                    m2 = mask_ref[mrow + 1:mrow + 2, c]
                    r1 = r_ref[top:top + 8, c] * m1
                    r2 = r_ref[top + 8:top + 16, c] * m2
                    e = jnp.concatenate([r1, r2, r1 * m2, jnp.zeros_like(r1)], axis=0)
                    e_hi, e_lo = split(e)
                    u = dot_nn(lhs, jnp.concatenate([e_hi, e_lo, e_hi], axis=0))
                    if q < GR // 16 - 1:
                        r_ref[top + 16:lo_row + GR, c] = r_ref[top + 16:lo_row + GR, c] + u[16:]
                    f_hi, f_lo = split(jnp.concatenate([r1, r2 + m2 * u[8:16]], axis=0))
                    wst_ref[16 * q:16 * q + 16, c] = f_hi
                    wst_ref[GR + 16 * q:GR + 16 * q + 16, c] = f_lo
            g_hh = jnp.concatenate([g_hi, g_hi], axis=1)
            for c in [slice(a,a+128) for a in range(0,n,128)]:
                upd = dot_nn(g_hh, wst_ref[:, c]) + dot_nn(g_lo, wst_ref[0:GR, c])
                if later:
                    r_ref[lo_row + GR:, c] = r_ref[lo_row + GR:, c] + upd[0:later]
                x_ref[:, c] = x_ref[:, c] + upd[later:]
        if t < 2:
            for i in range(4):
                at = (640, 128)[t] + i * 128
                z_ref[i * 128:(i + 1) * 128, :] = x_ref[:, at:at + 128].T
    out_ref[...] = x_ref[:, 0:128]


def vmem():
    return pl.BlockSpec(memory_space=pltpu.VMEM)


def index_call(core, order, device, values, errors):
    return pl.pallas_call(
        index_kernel,
        out_shape=jax.ShapeDtypeStruct((NOBS, 128), F32),
        in_specs=[pl.BlockSpec(memory_space=pltpu.SMEM)] + [vmem()] * 4,
        out_specs=vmem(),
        compiler_params=pltpu.CompilerParams(vmem_limit_bytes=VMEM_LIMIT),
        name="positions",
    )(core, order, device, values, errors)


def main_call(own, other, info, coupling):
    return pl.pallas_call(
        main_kernel,
        out_shape=jax.ShapeDtypeStruct((128, 128), F32),
        in_specs=[vmem()] * 4,
        out_specs=vmem(),
        scratch_shapes=[
            pltpu.VMEM((1024, 384), BF16),
            pltpu.VMEM((NOBS, 128), F32),
            pltpu.VMEM((128, 1152), F32),
            pltpu.VMEM((NOBS, 1152), F32),
            pltpu.VMEM((128, 1152), F32),
            pltpu.VMEM((NOBS, 128), F32),
            pltpu.VMEM((NOBS, 128), F32),
            pltpu.VMEM((NOBS, 128), F32),
            pltpu.VMEM((NOBS, 128), F32),
            pltpu.VMEM((1024, 128), F32),
            pltpu.VMEM((GR, 1024), BF16),
            pltpu.VMEM((2 * GR, 1152), BF16),
            pltpu.VMEM((128, NOBS), F32),
        ],
        compiler_params=pltpu.CompilerParams(vmem_limit_bytes=VMEM_LIMIT),
        name="filter",
    )(own, other, info, coupling)


def payload_of(ensemble, device, cell, coupling, me):
    flat = ensemble.reshape(AUG, -1)
    ids = lax.broadcasted_iota(jnp.int32, device.shape, 1)
    found = jnp.where(device == me, ids, NOBS)
    one = jnp.min(found, axis=1, keepdims=True)
    two = jnp.min(jnp.where(found == one, NOBS, found), axis=1, keepdims=True)
    pick = jnp.concatenate([one, two], axis=1)
    hot = pick[:, :, None] == ids[:, None, :]
    place = jnp.sum(jnp.where(hot, cell[:, None, :], 0), axis=2).reshape(-1)
    cols = jnp.where((pick.reshape(-1) < NOBS)[None, :], flat[:, place], 0.0).T
    flags = coupling.reshape(NB, NBLK)[0:2].reshape(-1).astype(F32)
    pad = jnp.zeros((13,), F32)
    return jnp.concatenate([
        cols[0], cols[5, 0:TAIL],
        cols[1], cols[5, TAIL:], pad,
        cols[2], flags[0:TAIL],
        cols[3], flags[TAIL:2 * TAIL],
        cols[4], flags[2 * TAIL:], pad,
    ])


def local(ensemble, obs_values, obs_errors, obs_device, obs_cell, obs_order, coupling):
    core = lax.axis_index("c")
    me = ((lax.axis_index("y") * 4 + lax.axis_index("x")) * 2 + core) * 8 + lax.axis_index("z")
    payload = payload_of(ensemble, obs_device, obs_cell, coupling, me)
    info = index_call(core.reshape(1), obs_order, obs_device, obs_values, obs_errors)
    group = lax.axis_size(("y", "x", "z"))
    own = lax.all_to_all(jnp.broadcast_to(payload[None], (group, PAY)), ("y", "x", "z"), 0, 0)
    other = lax.ppermute(own, "c", [(0, 1), (1, 0)])
    composite = main_call(own, other, info, coupling.reshape(NB, NBLK))
    flat = ensemble.reshape(AUG, -1)
    analysis = jnp.dot(composite[:AUG, :AUG], flat, precision=lax.Precision.HIGHEST)
    return analysis.reshape(ensemble.shape)


def solution(mesh):
    inner = Mesh(mesh.devices.reshape(8, 4, 2, 8), ("y", "x", "c", "z"))
    state = P(None, None, ("y", "x", "c"), "z")
    placed = (state, P(), P(), P(), P(), P(), state)
    return jax.shard_map(local, mesh=inner, in_specs=placed, out_specs=state, check_vma=False)
```

time: 1060 us -> 103 us (0.10)
  waiting for transfers between devices: 947 us -> 0.01 us
  blocking collectives: 0 us -> 44.3 us
  matrix products: 44.7 us -> 2.24 us
  Pallas kernels: 0 us -> 42.3 us
  other arithmetic: 31.3 us -> 2.73 us
  local copies, waits for them, and re-layouts: 22.2 us -> 5.99 us
  between operations: 13.9 us -> 0.08 us
    psum x3 -> x0, waiting for transfers between devices: 807 us -> none  [priors(): return lax.psum(contribution, ('lat', 'lon'))]
    all_gather x3 -> x0, waiting for transfers between devices: 141 us -> none  [local(): transforms = lax.all_gather(partial_maps, 'lon', axis=0, tiled=True)]
    all_to_all x0 -> x1, blocking collectives: none -> 44.3 us  [local(): lax.all_to_all(jnp.broadcast_to(payload[None], (group, PAY)), ('y', 'x',...]
    dot_general x69 -> x1, matrix products: 44.7 us -> 2.24 us  [local(): jnp.dot(composite[:AUG, :AUG], flat, precision=lax.Precision.HIGHEST)]
    pallas_call x0 -> x2, Pallas kernels: none -> 42.3 us  [the longest x1 38.7 us: main_call(): pl.pallas_call(main_kernel, out_shape=jax.ShapeDtypeStruct((128, 128), F3...]
    select_n x9 -> x2, other arithmetic: 13.4 us -> 0.08 us  [payload_of(): cols = jnp.where((pick.reshape(-1) < NOBS)[None, :], flat[:, place], 0.0).T]
    gather x18 -> x1, local copies, waits for them, and re-layouts: 13 us -> 0.55 us  [payload_of(): cols = jnp.where((pick.reshape(-1) < NOBS)[None, :], flat[:, place], 0.0).T]
  transfers between devices with their start and end apart: 6 -> 1, of which waited for: 6 -> 0; matrix products, arithmetic and copies ran while one was open for 1% -> 1% of each run, Pallas kernels for 0% -> 4%
where the time goes in v1:
time: 103 us; the launch traced here: 102 us
  blocking collectives  44.3 us (43%)
  Pallas kernels  42.3 us (41%)
  local copies, waits for them, and re-layouts  5.99 us (6%)
  starting transfers between devices  4.7 us (5%)
  other arithmetic  2.73 us (3%)
  matrix products  2.24 us (2%)
    all_to_all x1, blocking collectives, local(): lax.all_to_all(jnp.broadcast_to(payload[None], (group, PAY)), ('y', 'x',...  44.3 us
    pallas_call x1, Pallas kernels, main_call(): pl.pallas_call(main_kernel, out_shape=jax.ShapeDtypeStruct((128, 128), F3...  38.7 us
    ppermute x1, starting transfers between devices, local(): other = lax.ppermute(own, 'c', [(0, 1), (1, 0)])  4.7 us
    pallas_call x1, Pallas kernels, index_call(): pl.pallas_call(index_kernel, out_shape=jax.ShapeDtypeStruct((NOBS, 128),...  3.67 us
    unnamed x9, local copies, waits for them, and re-layouts  2.99 us
    dot_general x1, matrix products, local(): jnp.dot(composite[:AUG, :AUG], flat, precision=lax.Precision.HIGHEST)  2.24 us
  transfers between devices with their start and end apart: 1, of which 0 were waited for; matrix products, arithmetic and copies ran while one was open for 1% of the time, Pallas kernels for 4%

profile of v1, /device:TPU:1, one launch (start us, length us, event | category | flops | bytes accessed | tf_op | source)
XLA Modules:
  0.0 102.4 jit_solution(6086343391216140261)
XLA Ops:
  0.0 0.7 convert_reduce_fusion
  0.7 0.1 convert_element_type.7
  0.8 0.1 slice.47
  0.9 0.1 fusion.6
  0.9 0.8 fusion.4
  1.7 0.2 fusion.3
  2.0 0.1 copy.23
  2.1 0.1 lt.21
  2.2 0.1 copy.25
  2.3 0.9 fusion.2
  3.2 0.1 reshape.66
  3.3 1.5 %copy.24 = f32[81,10,2,128]{0,3,2,1:T(8,128)S(1)} copy(f32[81,10,2,128]{3,2,1,0:T(2,128)} %param.7) | data formatting | bytes 1658880 | tf_op args[0]
  4.8 0.6 gather_fusion
  5.4 0.1 broadcast_select_fusion
  5.5 0.1 slice_bitcast_fusion.5
  5.5 0.1 concatenate.7
  5.6 0.3 broadcast_in_dim.54
  6.0 0.0 copy-start.2
  6.0 44.3 %all_to_all.8 = f32[256,1,640]{2,1,0:T(1,128)S(1)} all-to-all(f32[256,1,640]{2,1,0:T(1,128)S(1)} %broadcast_in_dim.54), channel_id=1, replica_groups=mesh['y'=8,'x'=4,'c'=2,'z'=8] {'y','x','z'}, dimensions={0} | all-to-all | bytes 1310720 | tf_op jit(solution)/shard_map/all_to_all | solution.py:287
  50.4 0.0 copy-start
  50.4 4.7 %collective-permute-start = (f32[256,640]{1,0:T(8,128)S(1)}, f32[256,640]{1,0:T(8,128)S(1)}, u32[]{:S(2)}, u32[]{:S(2)}) collective-permute-start(f32[256,640]{1,0:T(8,128)S(1)} %bitcast.38), channel_id=1, source_target_pairs={{0,8},{8,0},{1,9},{9,1},{2,10},{10,2},{3,11},{11,3},{4,12},{12,4},... | collective-permute-start | bytes 1966088 | tf_op jit(solution)/shard_map/ppermute | solution.py:288
  55.1 0.0 copy-done.2
  55.1 0.6 copy.37
  55.7 3.7 %positions.1.info_ref = f32[512,128]{1,0:T(8,128)} custom-call(s32[1]{0:T(128)} %bitcast.11.core_ref, s32[3,512]{1,0:T(4,128)} %order_ref.1, s32[3,512]{1,0:T(4,128)} %device_ref.1, f32[3,512]{1,0:T(4,128)} %values_ref.1, f32[3,512]{1,0:T(4,128)} %errors_ref.1), custom_call_target="tpu_custom_call" | custom-call | tf_op jit(solution)/shard_map/positions/pallas_call | solution.py:224
  59.3 0.0 collective-permute-done.other_ref
  59.3 0.0 copy-start.1
  59.3 0.0 copy-done
  59.3 0.8 copy-done.1
  60.2 38.7 %filter.1 = f32[128,128]{1,0:T(8,128)} custom-call(f32[256,640]{1,0:T(8,128)} %bitcast.39, f32[256,640]{1,0:T(8,128)} %copy-done.1, f32[512,128]{1,0:T(8,128)} %positions.1.info_ref, s32[3,64]{1,0:T(4,128)} %bitcast.40), custom_call_target="tpu_custom_call" | custom-call | tf_op jit(solution)/shard_map/filter/pallas_call | solution.py:235
  98.8 2.2 %fusion = f32[81,10,2,128]{3,0,2,1:T(8,128)S(1)} fusion(f32[81,10,2,128]{0,3,2,1:T(8,128)S(1)} %copy.24, f32[128,128]{1,0:T(8,128)} %filter.1), kind=kOutput, calls=%fused_computation.1 | convolution fusion | flops 201553920 | bytes 1703936 | tf_op jit(solution)/shard_map/dot_general | solution.py:291
  101.1 1.3 %copy.27 = f32[81,10,2,128]{3,2,1,0:T(2,128)} copy(f32[81,10,2,128]{3,0,2,1:T(8,128)S(1)} %fusion) | data formatting | bytes 1658880 | tf_op jit(solution)/shard_map/dot_general | solution.py:291
  (8 shorter events, 0.1 us)
Async XLA Ops:
  6.0 49.1 %copy-start.2 = (s32[3,64,1,1]{1,3,2,0:T(1,128)S(1)}, s32[3,64,1,1]{1,3,2,0:T(1,128)}, u32[]{:S(2)}) copy-start(s32[3,64,1,1]{1,3,2,0:T(1,128)} %param.13) | copy-start | bytes 2308
  50.4 9.0 %copy-start = (f32[256,1,640]{2,0,1:T(8,128)}, f32[256,1,640]{2,0,1:T(8,128)S(1)}, u32[]{:S(2)}) copy-start(f32[256,1,640]{2,0,1:T(8,128)S(1)} %copy.36) | copy-start | bytes 1966084
  50.4 9.0 %collective-permute-start = (f32[256,640]{1,0:T(8,128)S(1)}, f32[256,640]{1,0:T(8,128)S(1)}, u32[]{:S(2)}, u32[]{:S(2)}) collective-permute-start(f32[256,640]{1,0:T(8,128)S(1)} %bitcast.38), channel_id=1, source_target_pairs={{0,8},{8,0},{1,9},{9,1},{2,10},{10,2},{3,11},{11,3},{4,12},{12,4},... | collective-permute-start | bytes 1966088 | tf_op jit(solution)/shard_map/ppermute | solution.py:288
  59.3 0.8 copy-start.1

commit v2 on v1

--- a/solution.py
+++ b/solution.py
@@ -16,6 +16,8 @@
 F32 = jnp.float32
 BF16 = jnp.bfloat16
 GR = 128
+XR = 96
+WIDE = 128
 VMEM_LIMIT = 56 * 1024 * 1024
 
 
@@ -48,7 +50,8 @@
         slot = jnp.zeros((1, NOBS), F32)
         for part in range(NOBS // rows):
             sub = iota((rows, NOBS), 0) + part * rows
-            own = jnp.sum(jnp.where(sub == lane, device_f, 0.0), axis=1, keepdims=True)
+            eye = iota((rows, rows), 0) == iota((rows, rows), 1)
+            own = jnp.sum(jnp.where(eye, device_f[:, part * rows:(part + 1) * rows], 0.0), axis=1, keepdims=True)
             same = jnp.where((own == device_f) & (sub < lane), 1.0, 0.0)
             slot = slot + jnp.sum(same, axis=0, keepdims=True)
         half = ((device >> 3) & 1) ^ core
@@ -68,7 +71,7 @@
 
 def main_kernel(own_ref, other_ref, info_ref, coupling_ref, out_ref,
                 buf_ref, z_ref, x_ref, r_ref, mask_ref, w_ref, vt_ref, wk_ref, vk_ref,
-                vx_ref, sx_ref, wst_ref, vv_ref):
+                vx_ref, sx_ref, wst_ref, vv_ref, sh_ref, sl_ref, keep_ref):
     lanes = iota((64, 128), 1)
     first = lanes == 0
     valid = lanes < AUG
@@ -110,6 +113,10 @@
     x_ref[:, 0:128] = jnp.where((iota((128, 128), 0) == iota((128, 128), 1))
                                     & (iota((128, 128), 0) < AUG), 1.0, 0.0)
 
+    i0 = iota((GR, 1024), 0)
+    i1 = iota((GR, 1024), 1)
+    ahead = (i0 >> 4) - (i1 >> 7)
+    keep_ref[...] = jnp.where((ahead > 0) | ((ahead == 0) & ((i0 & 15) >= 8) & ((i1 & 31) < 8)), 1.0, 0.0)
     for t in range(NB):
         n = (1152, 640, 128)[t]
         zs = [z_ref[i * 64:(i + 1) * 64, :] for i in range(OB)]
@@ -148,48 +155,46 @@
                                 coupling_ref[t:t + 1, :].astype(F32), 0.0), axis=1, keepdims=True)
         mask_ref[64 * (t % 2):64 * (t % 2) + 64, 0:128] = jnp.broadcast_to(own, (64, 128))
 
-        for g in range(NOBS // GR):
-            lo_row = g * GR
-            rows = slice(lo_row, lo_row + GR)
-            vg = vk_ref[rows, :]
-            v_hi, v_lo = split(vg)
-            v_hl = jnp.concatenate([v_hi, v_lo], axis=1)
-            wg_hi, wg_lo = w_hi[rows], w_lo[rows]
-            bt = dot_nt(v_hl, w_hh[rows]) + dot_nt(v_hi, wg_lo)
-            a0 = iota((GR, GR), 0)
-            a1 = iota((GR, GR), 1)
-            bt = jnp.where(((a0 >> 4) == (a1 >> 4)) & ((a0 & 15) < 8) & ((a1 & 15) >= 8), bt, 0.0)
-            b_hi, b_lo = split(bt)
-            v12 = dot_nn(jnp.concatenate([b_hi, b_hi], axis=1),
-                         jnp.concatenate([v_hi, v_lo], axis=0)) + dot_nn(b_lo, v_hi)
-            zero8 = jnp.zeros((8, 128), F32)
+        vk = vk_ref[...]
+        v_hi, v_lo = split(vk)
+        v_hl = jnp.concatenate([v_hi, v_lo], axis=1)
+        groups = [slice(g * GR, g * GR + GR) for g in range(NOBS // GR)]
+        bts = [dot_nt(v_hl[r], w_hh[r]) + dot_nt(v_hi[r], w_lo[r]) for r in groups]
+        a0 = iota((GR, GR), 0)
+        a1 = iota((GR, GR), 1)
+        pairs = ((a0 >> 4) == (a1 >> 4)) & ((a0 & 15) < 8) & ((a1 & 15) >= 8)
+        v12s = []
+        for r, bt in zip(groups, bts):
+            b_hi, b_lo = split(jnp.where(pairs, bt, 0.0))
+            v12s.append(dot_nn(jnp.concatenate([b_hi, b_hi], axis=1),
+                               jnp.concatenate([v_hi[r], v_lo[r]], axis=0)) + dot_nn(b_lo, v_hi[r]))
+        for g in range(NOBS // GR - 1):
+            r = groups[g]
+            s_hi, s_lo = split(dot_nt(w_hh[r.stop:], v_hl[r]) + dot_nt(w_lo[r.stop:], v_hi[r]))
+            sh_ref[r.stop:, r] = s_hi
+            sl_ref[r.stop:, r] = s_lo
+        zero8 = jnp.zeros((8, 128), F32)
+        for g, r in enumerate(groups):
+            vg, v12 = vk[r], v12s[g]
             for q in range(GR // 16):
                 piece = jnp.concatenate([vg[16 * q:16 * q + 8], vg[16 * q + 8:16 * q + 16],
                                          v12[16 * q:16 * q + 8], zero8], axis=0)
                 for rep in range(4):
                     vx_ref[q * 128 + rep * 32:q * 128 + rep * 32 + 32, :] = piece
             e_hi, e_lo = split(vx_ref[...])
-            sx = dot_nt(w_hh[rows], jnp.concatenate([e_hi, e_lo], axis=1)) + dot_nt(wg_lo, e_hi)
-            s_hi, s_lo = split(sx)
-            i0 = iota((GR, 1024), 0)
-            i1 = iota((GR, 1024), 1)
-            ahead = (i0 >> 4) - (i1 >> 7)
-            keep = (ahead > 0) | ((ahead == 0) & ((i0 & 15) >= 8) & ((i1 & 31) < 8))
-            sx = jnp.where((i1 & 127) < 64, s_hi.astype(F32), s_lo.astype(F32))
-            sx_ref[...] = jnp.where(keep, sx, 0.0).astype(BF16)
-            later = NOBS - lo_row - GR
-            g_hi, g_lo = split(vv_ref[:, rows])
-            if later:
-                sg = dot_nt(w_hh[lo_row + GR:], v_hl) + dot_nt(w_lo[lo_row + GR:], v_hi)
-                sg_hi, sg_lo = split(sg)
-                g_hi = jnp.concatenate([sg_hi, g_hi], axis=0)
-                g_lo = jnp.concatenate([sg_lo, g_lo], axis=0)
-
-            chunks = [slice(c, min(c + 256, n)) for c in range(0, n, 256)]
+            sx = dot_nt(w_hh[r], jnp.concatenate([e_hi, e_lo], axis=1)) + dot_nt(w_lo[r], e_hi)
+            sx = sx * keep_ref[...]
+            s_hi = sx.astype(BF16).astype(F32)
+            sx_ref[r, :] = jnp.where((iota((GR, 1024), 1) & 127) < 64, s_hi, sx - s_hi).astype(BF16)
+
+        chunks = [slice(c, min(c + 256, n)) for c in range(0, n, 256)]
+        wide = [slice(c, min(c + WIDE, n)) for c in range(0, n, WIDE)]
+        for g, rows in enumerate(groups):
+            lo_row = g * GR
             for q in range(GR // 16):
                 top = lo_row + 16 * q
                 mrow = 64 * (t % 2) + top // 8
-                lhs = sx_ref[16 * q:GR, q * 128:q * 128 + 96]
+                lhs = sx_ref[top:lo_row + GR, q * 128:q * 128 + 96]
                 for c in chunks:
                     m1 = mask_ref[mrow:mrow + 1, c]
                     m2 = mask_ref[mrow + 1:mrow + 2, c]
@@ -203,12 +208,17 @@
                     f_hi, f_lo = split(jnp.concatenate([r1, r2 + m2 * u[8:16]], axis=0))
                     wst_ref[16 * q:16 * q + 16, c] = f_hi
                     wst_ref[GR + 16 * q:GR + 16 * q + 16, c] = f_lo
+            later = NOBS - lo_row - GR
+            g_hi, g_lo = split(vv_ref[0:XR, rows])
+            if later:
+                g_hi = jnp.concatenate([sh_ref[lo_row + GR:, rows], g_hi], axis=0)
+                g_lo = jnp.concatenate([sl_ref[lo_row + GR:, rows], g_lo], axis=0)
             g_hh = jnp.concatenate([g_hi, g_hi], axis=1)
-            for c in [slice(a,a+128) for a in range(0,n,128)]:
+            for c in wide:
                 upd = dot_nn(g_hh, wst_ref[:, c]) + dot_nn(g_lo, wst_ref[0:GR, c])
                 if later:
                     r_ref[lo_row + GR:, c] = r_ref[lo_row + GR:, c] + upd[0:later]
-                x_ref[:, c] = x_ref[:, c] + upd[later:]
+                x_ref[0:XR, c] = x_ref[0:XR, c] + upd[later:]
         if t < 2:
             for i in range(4):
                 at = (640, 128)[t] + i * 128
@@ -248,47 +258,86 @@
             pltpu.VMEM((NOBS, 128), F32),
             pltpu.VMEM((NOBS, 128), F32),
             pltpu.VMEM((1024, 128), F32),
-            pltpu.VMEM((GR, 1024), BF16),
+            pltpu.VMEM((NOBS, 1024), BF16),
             pltpu.VMEM((2 * GR, 1152), BF16),
             pltpu.VMEM((128, NOBS), F32),
+            pltpu.VMEM((NOBS, NOBS), BF16),
+            pltpu.VMEM((NOBS, NOBS), BF16),
+            pltpu.VMEM((GR, 1024), F32),
         ],
         compiler_params=pltpu.CompilerParams(vmem_limit_bytes=VMEM_LIMIT),
         name="filter",
     )(own, other, info, coupling)
 
 
-def payload_of(ensemble, device, cell, coupling, me):
-    flat = ensemble.reshape(AUG, -1)
-    ids = lax.broadcasted_iota(jnp.int32, device.shape, 1)
-    found = jnp.where(device == me, ids, NOBS)
-    one = jnp.min(found, axis=1, keepdims=True)
-    two = jnp.min(jnp.where(found == one, NOBS, found), axis=1, keepdims=True)
-    pick = jnp.concatenate([one, two], axis=1)
-    hot = pick[:, :, None] == ids[:, None, :]
-    place = jnp.sum(jnp.where(hot, cell[:, None, :], 0), axis=2).reshape(-1)
-    cols = jnp.where((pick.reshape(-1) < NOBS)[None, :], flat[:, place], 0.0).T
-    flags = coupling.reshape(NB, NBLK)[0:2].reshape(-1).astype(F32)
-    pad = jnp.zeros((13,), F32)
-    return jnp.concatenate([
-        cols[0], cols[5, 0:TAIL],
-        cols[1], cols[5, TAIL:], pad,
-        cols[2], flags[0:TAIL],
-        cols[3], flags[TAIL:2 * TAIL],
-        cols[4], flags[2 * TAIL:], pad,
-    ])
+def payload_kernel(me_ref, device_ref, cell_ref, flags_ref, ensemble_ref, out_ref,
+                   tile_ref, pay_ref, last_ref, sems):
+    me = me_ref[0]
+    lane = iota((1, NOBS), 1)
+    copies, hots = [], []
+    lane128 = iota((8, 256), 1)
+    for t in range(NB):
+        found = jnp.where(device_ref[t:t + 1, :] == me, lane, NOBS)
+        one = jnp.min(found)
+        two = jnp.min(jnp.where(found == one, NOBS, found))
+        for s, pick in enumerate((one, two)):
+            at = 2 * t + s
+            cell = jnp.max(jnp.where(lane == pick, cell_ref[t:t + 1, :], 0))
+            copy = pltpu.make_async_copy(ensemble_ref.at[:, cell >> 8], tile_ref.at[at], sems.at[at])
+            copy.start()
+            copies.append(copy)
+            spot = jnp.where(pick < NOBS, cell & 255, 256)
+            hots.append(jnp.where(lane128 == spot, 1.0, 0.0).astype(BF16))
+    pay_ref[...] = jnp.zeros_like(pay_ref)
+    last_ref[...] = jnp.zeros_like(last_ref)
+    for at in range(2 * NB):
+        copies[at].wait()
+        pair = jnp.concatenate([tile_ref[at, :, 0, :], tile_ref[at, :, 1, :]], axis=1)
+        hi, mid = split(pair)
+        rest = (pair - hi.astype(F32) - mid.astype(F32)).astype(BF16)
+        col = dot_nt(hots[at], hi) + dot_nt(hots[at], mid) + dot_nt(hots[at], rest)
+        if at < 5:
+            pay_ref[:, 128 * at:128 * at + AUG] = col
+        else:
+            last_ref[:, 0:AUG] = col
+    lane = iota((8, 128), 1)
+    last = last_ref[...]
+    flags = jnp.broadcast_to(flags_ref[...].astype(F32), (8, 128))
+    tails = [pltpu.roll(last, AUG, 1), pltpu.roll(last, AUG - TAIL, 1), pltpu.roll(flags, AUG, 1),
+             pltpu.roll(flags, AUG - TAIL, 1), pltpu.roll(flags, (AUG - 2 * TAIL) % 128, 1)]
+    for at in range(5):
+        row = jnp.where(lane < AUG, pay_ref[:, 128 * at:128 * at + 128], tails[at])
+        out_ref[:, 128 * at:128 * at + 128] = jnp.concatenate([row] * 32, axis=0)
+
+
+def payload_call(me, device, cell, flags, ensemble):
+    return pl.pallas_call(
+        payload_kernel,
+        out_shape=jax.ShapeDtypeStruct((256, PAY), F32),
+        in_specs=[pl.BlockSpec(memory_space=pltpu.SMEM)] + [vmem()] * 3 + [pl.BlockSpec(memory_space=pl.ANY)],
+        out_specs=vmem(),
+        scratch_shapes=[
+            pltpu.VMEM((6, AUG, 2, 128), F32),
+            pltpu.VMEM((8, PAY), F32),
+            pltpu.VMEM((8, 128), F32),
+            pltpu.SemaphoreType.DMA((6,)),
+        ],
+        compiler_params=pltpu.CompilerParams(vmem_limit_bytes=VMEM_LIMIT),
+        name="payload",
+    )(me, device, cell, flags, ensemble)
 
 
 def local(ensemble, obs_values, obs_errors, obs_device, obs_cell, obs_order, coupling):
     core = lax.axis_index("c")
     me = ((lax.axis_index("y") * 4 + lax.axis_index("x")) * 2 + core) * 8 + lax.axis_index("z")
-    payload = payload_of(ensemble, obs_device, obs_cell, coupling, me)
+    flags = coupling.reshape(1, NB * NBLK)
+    payload = payload_call(me.reshape(1), obs_device, obs_cell, flags[:, 0:2 * NBLK], ensemble)
     info = index_call(core.reshape(1), obs_order, obs_device, obs_values, obs_errors)
-    group = lax.axis_size(("y", "x", "z"))
-    own = lax.all_to_all(jnp.broadcast_to(payload[None], (group, PAY)), ("y", "x", "z"), 0, 0)
+    own = lax.all_to_all(payload, ("y", "x", "z"), 0, 0, tiled=True)
     other = lax.ppermute(own, "c", [(0, 1), (1, 0)])
     composite = main_call(own, other, info, coupling.reshape(NB, NBLK))
     flat = ensemble.reshape(AUG, -1)
-    analysis = jnp.dot(composite[:AUG, :AUG], flat, precision=lax.Precision.HIGHEST)
+    analysis = jnp.dot(composite[:AUG, :AUG], flat, precision=lax.Precision.HIGH)
     return analysis.reshape(ensemble.shape)
 
 

time: 103 us -> 102 us (level)
  other arithmetic: 2.73 us -> 0.02 us
  Pallas kernels: 42.3 us -> 43.9 us
  local copies, waits for them, and re-layouts: 5.99 us -> 7.08 us
    pallas_call x0 -> x1, Pallas kernels: none -> 4.55 us  [payload_call(): pl.pallas_call(payload_kernel, out_shape=jax.ShapeDtypeStruct((256, PAY),...]
    pallas_call x1, Pallas kernels: 38.7 us -> 35.7 us  [main_call(): pl.pallas_call(main_kernel, out_shape=jax.ShapeDtypeStruct((128, 128), F3...]
    all_to_all x0 -> x1, local copies, waits for them, and re-layouts: none -> 1.76 us  [local(): own = lax.all_to_all(payload, ('y', 'x', 'z'), 0, 0, tiled=True)]
    unnamed x9 -> x10, local copies, waits for them, and re-layouts: 2.99 us -> 2.16 us
  transfers between devices with their start and end apart: 1 -> 1, of which waited for: 0 -> 0; matrix products, arithmetic and copies ran while one was open for 1% -> 2% of each run, Pallas kernels for 4% -> 4%
where the time goes in v2:
time: 102 us
  blocking collectives  44.3 us (43%)
  Pallas kernels  43.9 us (43%)
  local copies, waits for them, and re-layouts  7.08 us (7%)
  starting transfers between devices  4.84 us (5%)
  matrix products  1.3 us (1%)
    all_to_all x1, blocking collectives, local(): own = lax.all_to_all(payload, ('y', 'x', 'z'), 0, 0, tiled=True)  44.3 us
    pallas_call x1, Pallas kernels, main_call(): pl.pallas_call(main_kernel, out_shape=jax.ShapeDtypeStruct((128, 128), F3...  35.7 us
    ppermute x1, starting transfers between devices, local(): other = lax.ppermute(own, 'c', [(0, 1), (1, 0)])  4.84 us
    pallas_call x1, Pallas kernels, payload_call(): pl.pallas_call(payload_kernel, out_shape=jax.ShapeDtypeStruct((256, PAY),...  4.55 us
    pallas_call x1, Pallas kernels, index_call(): pl.pallas_call(index_kernel, out_shape=jax.ShapeDtypeStruct((NOBS, 128),...  3.65 us
    unnamed x10, local copies, waits for them, and re-layouts  2.16 us
  transfers between devices with their start and end apart: 1, of which 0 were waited for; matrix products, arithmetic and copies ran while one was open for 2% of the time, Pallas kernels for 4%

profile of v2, /device:TPU:1, one launch (start us, length us, event | category | flops | bytes accessed | tf_op | source)
XLA Modules:
  0.0 101.6 jit_solution(997612067904643103)
XLA Ops:
  0.0 0.0 copy-start.3
  0.0 0.7 copy-done.3
  0.7 0.1 reshape.20
  0.8 0.5 slice.8.flags_ref
  1.3 4.5 %payload.1 = f32[256,640]{1,0:T(8,128)} custom-call(s32[1]{0:T(128)} %bitcast.me_ref, s32[3,512]{1,0:T(4,128)} %device_ref.3, s32[3,512]{1,0:T(4,128)} %cell_ref.1, s32[1,128]{1,0:T(1,128)} %slice.8.flags_ref, f32[81,10,2,128]{3,2,1,0:T(2,128)} %ensemble_ref.1), custom_call_target="tpu_custom_call" | custom-call | tf_op jit(solution)/shard_map/payload/pallas_call | solution.py:314
  5.9 1.8 %copy.11 = f32[256,1,640]{2,1,0:T(1,128)S(1)} copy(f32[256,1,640]{2,0,1:T(8,128)} %bitcast.20) | data formatting | bytes 1310720 | tf_op jit(solution)/shard_map/all_to_all | solution.py:336
  7.7 44.3 %all_to_all.11 = f32[256,1,640]{2,1,0:T(1,128)S(1)} all-to-all(f32[256,1,640]{2,1,0:T(1,128)S(1)} %copy.11), channel_id=1, replica_groups=mesh['y'=8,'x'=4,'c'=2,'z'=8] {'y','x','z'}, dimensions={0} | all-to-all | bytes 1310720 | tf_op jit(solution)/shard_map/all_to_all | solution.py:336
  52.0 0.0 copy-start
  52.0 0.0 copy-start.1
  52.0 4.8 %collective-permute-start = (f32[256,640]{1,0:T(8,128)S(1)}, f32[256,640]{1,0:T(8,128)S(1)}, u32[]{:S(2)}, u32[]{:S(2)}) collective-permute-start(f32[256,640]{1,0:T(8,128)S(1)} %bitcast.18), channel_id=1, source_target_pairs={{0,8},{8,0},{1,9},{9,1},{2,10},{10,2},{3,11},{11,3},{4,12},{12,4},... | collective-permute-start | bytes 1966088 | tf_op jit(solution)/shard_map/ppermute | solution.py:337
  56.9 0.6 copy.22
  57.5 0.0 copy-done
  57.5 0.7 reshape.23
  58.2 0.0 copy-done.1
  58.2 0.5 dot_general.8
  58.7 3.7 %positions.1.info_ref = f32[512,128]{1,0:T(8,128)} custom-call(s32[1]{0:T(128)} %bitcast.2.core_ref, s32[3,512]{1,0:T(4,128)} %order_ref.1, s32[3,512]{1,0:T(4,128)} %device_ref.3, f32[3,512]{1,0:T(4,128)} %values_ref.1, f32[3,512]{1,0:T(4,128)} %errors_ref.1), custom_call_target="tpu_custom_call" | custom-call | tf_op jit(solution)/shard_map/positions/pallas_call | solution.py:234
  62.4 0.0 collective-permute-done.other_ref
  62.4 0.0 copy-start.2
  62.4 0.8 copy-done.2
  63.2 35.7 %filter.1 = f32[128,128]{1,0:T(8,128)} custom-call(f32[256,640]{1,0:T(8,128)} %bitcast.19, f32[256,640]{1,0:T(8,128)} %copy-done.2, f32[512,128]{1,0:T(8,128)} %positions.1.info_ref, s32[3,64]{1,0:T(4,128)} %bitcast.21), custom_call_target="tpu_custom_call" | custom-call | tf_op jit(solution)/shard_map/filter/pallas_call | solution.py:245
  99.0 1.3 %fusion = f32[81,10,2,128]{3,0,2,1:T(8,128)S(1)} fusion(f32[10,2,128,81]{2,1,0,3:T(2,128)S(1)} %dot_general.8, f32[128,128]{1,0:T(8,128)} %filter.1), kind=kOutput, calls=%fused_computation | convolution fusion | flops 100776960 | bytes 1703936 | tf_op jit(solution)/shard_map/dot_general | solution.py:340
  100.3 1.3 %copy.13 = f32[81,10,2,128]{3,2,1,0:T(2,128)} copy(f32[81,10,2,128]{3,0,2,1:T(8,128)S(1)} %fusion) | data formatting | bytes 1658880 | tf_op jit(solution)/shard_map/dot_general | solution.py:340
  (2 shorter events, 0.1 us)
Async XLA Ops:
  0.0 0.7 copy-start.3
  52.0 5.5 %copy-start = (f32[81,10,2,128]{3,2,1,0:T(2,128)S(1)}, f32[81,10,2,128]{3,2,1,0:T(2,128)}, u32[]{:S(2)}) copy-start(f32[81,10,2,128]{3,2,1,0:T(2,128)} %ensemble_ref.1) | copy-start | bytes 2488324
  52.0 6.1 %copy-start.1 = (f32[256,1,640]{2,0,1:T(8,128)}, f32[256,1,640]{2,0,1:T(8,128)S(1)}, u32[]{:S(2)}) copy-start(f32[256,1,640]{2,0,1:T(8,128)S(1)} %copy.21) | copy-start | bytes 1966084
  52.0 10.3 %collective-permute-start = (f32[256,640]{1,0:T(8,128)S(1)}, f32[256,640]{1,0:T(8,128)S(1)}, u32[]{:S(2)}, u32[]{:S(2)}) collective-permute-start(f32[256,640]{1,0:T(8,128)S(1)} %bitcast.18), channel_id=1, source_target_pairs={{0,8},{8,0},{1,9},{9,1},{2,10},{10,2},{3,11},{11,3},{4,12},{12,4},... | collective-permute-start | bytes 1966088 | tf_op jit(solution)/shard_map/ppermute | solution.py:337
  62.4 0.8 copy-start.2

commit v3 on v2

--- a/solution.py
+++ b/solution.py
@@ -43,30 +43,37 @@
     core = core_ref[0]
     rows = 128
     lane = iota((rows, NOBS), 1)
+    eye = iota((rows, rows), 0) == iota((rows, rows), 1)
+    tables = []
     for t in range(NB):
-        order = order_ref[t:t + 1, :].astype(F32)
         device = device_ref[t:t + 1, :]
         device_f = device.astype(F32)
         slot = jnp.zeros((1, NOBS), F32)
         for part in range(NOBS // rows):
             sub = iota((rows, NOBS), 0) + part * rows
-            eye = iota((rows, rows), 0) == iota((rows, rows), 1)
             own = jnp.sum(jnp.where(eye, device_f[:, part * rows:(part + 1) * rows], 0.0), axis=1, keepdims=True)
             same = jnp.where((own == device_f) & (sub < lane), 1.0, 0.0)
             slot = slot + jnp.sum(same, axis=0, keepdims=True)
         half = ((device >> 3) & 1) ^ core
-        place = half * 256 + (device >> 4) * 8 + (device & 7)
-        place = place.astype(F32) + slot * 512.0
-        values = values_ref[t:t + 1, :]
-        errors = errors_ref[t:t + 1, :]
-        for part in range(NOBS // rows):
-            sub = iota((rows, NOBS), 0) + part * rows
-            source = (sub & 63) * OB + (sub >> 6)
+        place = (device >> 4) * 8 + (device & 7)
+        pieces = [half.astype(F32) * 256.0, place.astype(F32), jnp.zeros((1, NOBS), F32)]
+        for ref in (values_ref, errors_ref):
+            full = ref[t:t + 1, :]
+            hi = full.astype(BF16).astype(F32)
+            mid = (full - hi).astype(BF16).astype(F32)
+            pieces += [hi, mid, full - hi - mid]
+        tables.append(jnp.concatenate(pieces + [slot, jnp.zeros((6, NOBS), F32)], axis=0).astype(BF16))
+    for part in range(NOBS // rows):
+        sub = iota((rows, NOBS), 0) + part * rows
+        source = (sub & 63) * OB + (sub >> 6)
+        for t in range(NB):
+            order = order_ref[t:t + 1, :].astype(F32)
             ident = jnp.sum(jnp.where(source == lane, order, 0.0), axis=1, keepdims=True)
-            hot = ident == lane.astype(F32)
-            for c, table in enumerate((place, values, errors)):
-                col = jnp.sum(jnp.where(hot, table, 0.0), axis=1, keepdims=True)
-                out_ref[part * rows:(part + 1) * rows, t * 3 + c:t * 3 + c + 1] = col
+            hot = jnp.where(ident == lane.astype(F32), 1.0, 0.0).astype(BF16)
+            got = dot_nt(hot, tables[t])
+            out_ref[part * rows:(part + 1) * rows, t * 16:t * 16 + 16] = got
+        got = out_ref[part * rows:(part + 1) * rows, :]
+        out_ref[part * rows:(part + 1) * rows, :] = got + pltpu.roll(got, 127, 1) + pltpu.roll(got, 126, 1)
 
 
 def main_kernel(own_ref, other_ref, info_ref, coupling_ref, out_ref,
@@ -87,29 +94,30 @@
                 pieces = [ref[:, 512:640], jnp.where(lane < TAIL, head, tail)]
             for s in range(2):
                 hi, lo = split(pieces[s])
-                buf_ref[s * 512 + part:s * 512 + part + 256, 0:128] = hi
-                buf_ref[s * 512 + part:s * 512 + part + 256, 128:256] = lo
+                buf_ref[part:part + 256, 256 * s:256 * s + 128] = hi
+                buf_ref[part:part + 256, 256 * s + 128:256 * s + 256] = lo
             if t == 0:
                 lane = iota((256, 128), 1)
                 c0 = pltpu.roll(ref[:, 256:384], 128 - AUG, 1)
                 c1 = pltpu.roll(ref[:, 384:512], 128 - AUG + TAIL, 1)
                 c2 = pltpu.roll(ref[:, 512:640], (128 - AUG + 2 * TAIL) % 128, 1)
                 flags = jnp.where(lane < TAIL, c0, jnp.where(lane < 2 * TAIL, c1, c2)).astype(BF16)
-                buf_ref[part:part + 256, 256:384] = flags
-                buf_ref[512 + part:512 + part + 256, 256:384] = flags
-        width = 256 if t == 0 else 384
+                buf_ref[part:part + 256, 512:640] = flags
+        width = 512 if t == 0 else 640
         for i in range(4):
             rows = slice(i * 128, (i + 1) * 128)
-            place = info_ref[rows, 3 * t:3 * t + 1].astype(jnp.int32)
-            hot = jnp.where(place == iota((128, 1024), 1), 1.0, 0.0).astype(BF16)
+            place = info_ref[rows, 16 * t:16 * t + 1].astype(jnp.int32)
+            second = info_ref[rows, 16 * t + 9:16 * t + 10] > 0.5
+            hot = jnp.where(place == iota((128, 512), 1), 1.0, 0.0).astype(BF16)
             got = dot_nn(hot, buf_ref[:, 0:width])
-            z = jnp.where(iota((128, 128), 1) < AUG, got[:, 0:128] + got[:, 128:256], 0.0)
+            z = jnp.where(second, got[:, 256:384] + got[:, 384:512], got[:, 0:128] + got[:, 128:256])
+            z = jnp.where(iota((128, 128), 1) < AUG, z, 0.0)
             if t == 0:
                 z_ref[rows, :] = z
             else:
                 at = (0, 640, 128)[t] + i * 128
                 x_ref[:, at:at + 128] = z.T
-                mask_ref[:, at:at + 128] = got[:, 256:384].T
+                mask_ref[:, at:at + 128] = got[:, 512:640].T
     x_ref[:, 0:128] = jnp.where((iota((128, 128), 0) == iota((128, 128), 1))
                                     & (iota((128, 128), 0) < AUG), 1.0, 0.0)
 
@@ -120,23 +128,34 @@
     for t in range(NB):
         n = (1152, 640, 128)[t]
         zs = [z_ref[i * 64:(i + 1) * 64, :] for i in range(OB)]
-        hs, vs, ws = [], [], []
+        shrinks, ws = [], []
+        hs = [jnp.where(first, 0.0, z) for z in zs]
+        gram = [[jnp.sum(hs[j] * hs[l], axis=1, keepdims=True) for l in range(j + 1)] for j in range(OB)]
+        cross = [[None] * OB for _ in range(OB)]
         for i in range(OB):
             p = zs[i]
-            value = info_ref[i * 64:(i + 1) * 64, 3 * t + 1:3 * t + 2]
-            error = info_ref[i * 64:(i + 1) * 64, 3 * t + 2:3 * t + 3]
+            value = info_ref[i * 64:(i + 1) * 64, 16 * t + 3:16 * t + 4]
+            error = info_ref[i * 64:(i + 1) * 64, 16 * t + 6:16 * t + 7]
             h = jnp.where(first, 0.0, p)
-            q = jnp.sum(h * h, axis=1, keepdims=True) / (AUG - 2) + error
+            total = gram[i][i]
+            q = total / (AUG - 2) + error
             c = 1.0 / ((AUG - 2) * q)
-            a = 1.0 / (1.0 + jnp.sqrt(error / q))
-            v = jnp.where(first, c * (value - p[:, 0:1]), -(a * c) * h)
+            shrink = c / (1.0 + jnp.sqrt(error / q))
+            v = jnp.where(first, c * (value - p[:, 0:1]), -shrink * h)
             v = jnp.where(valid, v, 0.0)
+            both = shrink * (2.0 - shrink * total)
             for j in range(i + 1, OB):
-                zs[j] = zs[j] + v * jnp.sum(h * zs[j], axis=1, keepdims=True)
+                along = gram[j][i]
+                zs[j] = zs[j] + v * along
+                cross[j][i] = along * (1.0 - shrink * total)
+                for l in range(i):
+                    cross[j][l] = cross[j][l] - shrink * cross[i][l] * along
+                for l in range(i + 1, j + 1):
+                    gram[j][l] = gram[j][l] - both * along * gram[l][i]
             w = h
             for l in range(i):
-                w = w + ws[l] * jnp.sum(h * vs[l], axis=1, keepdims=True)
-            vs.append(v)
+                w = w - ws[l] * (shrinks[l] * cross[i][l])
+            shrinks.append(shrink)
             ws.append(w)
             w_ref[i * 64:(i + 1) * 64, :] = w
             vt_ref[i * 64:(i + 1) * 64, :] = v
@@ -248,7 +267,7 @@
         in_specs=[vmem()] * 4,
         out_specs=vmem(),
         scratch_shapes=[
-            pltpu.VMEM((1024, 384), BF16),
+            pltpu.VMEM((NOBS, 640), BF16),
             pltpu.VMEM((NOBS, 128), F32),
             pltpu.VMEM((128, 1152), F32),
             pltpu.VMEM((NOBS, 1152), F32),
@@ -277,16 +296,17 @@
     copies, hots = [], []
     lane128 = iota((8, 256), 1)
     for t in range(NB):
-        found = jnp.where(device_ref[t:t + 1, :] == me, lane, NOBS)
-        one = jnp.min(found)
-        two = jnp.min(jnp.where(found == one, NOBS, found))
-        for s, pick in enumerate((one, two)):
+        mine = device_ref[t:t + 1, :] == me
+        key = lane * 4096 + cell_ref[t:t + 1, :]
+        one = jnp.min(jnp.where(mine, key, NOBS * 4096))
+        two = jnp.max(jnp.where(mine, key, -1))
+        for s, (pick, held) in enumerate(((one, one < NOBS * 4096), (two, two > one))):
             at = 2 * t + s
-            cell = jnp.max(jnp.where(lane == pick, cell_ref[t:t + 1, :], 0))
+            cell = jnp.where(held, pick & 4095, 0)
             copy = pltpu.make_async_copy(ensemble_ref.at[:, cell >> 8], tile_ref.at[at], sems.at[at])
             copy.start()
             copies.append(copy)
-            spot = jnp.where(pick < NOBS, cell & 255, 256)
+            spot = jnp.where(held, cell & 255, 256)
             hots.append(jnp.where(lane128 == spot, 1.0, 0.0).astype(BF16))
     pay_ref[...] = jnp.zeros_like(pay_ref)
     last_ref[...] = jnp.zeros_like(last_ref)
@@ -307,13 +327,13 @@
              pltpu.roll(flags, AUG - TAIL, 1), pltpu.roll(flags, (AUG - 2 * TAIL) % 128, 1)]
     for at in range(5):
         row = jnp.where(lane < AUG, pay_ref[:, 128 * at:128 * at + 128], tails[at])
-        out_ref[:, 128 * at:128 * at + 128] = jnp.concatenate([row] * 32, axis=0)
+        out_ref[:, 128 * at:128 * at + 128] = row
 
 
 def payload_call(me, device, cell, flags, ensemble):
     return pl.pallas_call(
         payload_kernel,
-        out_shape=jax.ShapeDtypeStruct((256, PAY), F32),
+        out_shape=jax.ShapeDtypeStruct((8, PAY), F32),
         in_specs=[pl.BlockSpec(memory_space=pltpu.SMEM)] + [vmem()] * 3 + [pl.BlockSpec(memory_space=pl.ANY)],
         out_specs=vmem(),
         scratch_shapes=[
@@ -333,7 +353,8 @@
     flags = coupling.reshape(1, NB * NBLK)
     payload = payload_call(me.reshape(1), obs_device, obs_cell, flags[:, 0:2 * NBLK], ensemble)
     info = index_call(core.reshape(1), obs_order, obs_device, obs_values, obs_errors)
-    own = lax.all_to_all(payload, ("y", "x", "z"), 0, 0, tiled=True)
+    group = lax.axis_size(("y", "x", "z"))
+    own = lax.all_to_all(jnp.broadcast_to(payload[0:1], (group, PAY)), ("y", "x", "z"), 0, 0, tiled=True)
     other = lax.ppermute(own, "c", [(0, 1), (1, 0)])
     composite = main_call(own, other, info, coupling.reshape(NB, NBLK))
     flat = ensemble.reshape(AUG, -1)

time: 102 us -> 99.9 us (0.979)
  Pallas kernels: 43.9 us -> 42.6 us
    all_to_all x1 -> x0, local copies, waits for them, and re-layouts: 1.76 us -> none  [local(): own = lax.all_to_all(payload, ('y', 'x', 'z'), 0, 0, tiled=True)]
  transfers between devices with their start and end apart: 1 -> 1, of which waited for: 0 -> 0; matrix products, arithmetic and copies ran while one was open for 2% -> 2% of each run, Pallas kernels for 4% -> 3%
where the time goes in v3:
time: 99.9 us; the launch traced here: 99.5 us
  blocking collectives  44.3 us (44%)
  Pallas kernels  42.6 us (43%)
  local copies, waits for them, and re-layouts  6.34 us (6%)
  starting transfers between devices  4.84 us (5%)
  matrix products  1.3 us (1%)
    all_to_all x1, blocking collectives, local(): lax.all_to_all(jnp.broadcast_to(payload[0:1], (group, PAY)), ('y', 'x', '...  44.3 us
    pallas_call x1, Pallas kernels, main_call(): pl.pallas_call(main_kernel, out_shape=jax.ShapeDtypeStruct((128, 128), F3...  35.5 us
    ppermute x1, starting transfers between devices, local(): other = lax.ppermute(own, 'c', [(0, 1), (1, 0)])  4.84 us
    pallas_call x1, Pallas kernels, payload_call(): pl.pallas_call(payload_kernel, out_shape=jax.ShapeDtypeStruct((8, PAY), F...  3.98 us
    pallas_call x1, Pallas kernels, index_call(): pl.pallas_call(index_kernel, out_shape=jax.ShapeDtypeStruct((NOBS, 128),...  3.04 us
    unnamed x10, local copies, waits for them, and re-layouts  2.14 us
  transfers between devices with their start and end apart: 1, of which 0 were waited for; matrix products, arithmetic and copies ran while one was open for 2% of the time, Pallas kernels for 3%

profile of v3, /device:TPU:1, one launch (start us, length us, event | category | flops | bytes accessed | tf_op | source)
XLA Modules:
  0.0 99.5 jit_solution(8813899610938754561)
XLA Ops:
  0.0 0.0 copy-start.3
  0.0 0.7 copy-done.3
  0.7 0.1 reshape.24
  0.8 0.5 slice.15.flags_ref
  1.3 4.0 %payload.1 = f32[8,640]{1,0:T(8,128)} custom-call(s32[1]{0:T(128)} %bitcast.me_ref, s32[3,512]{1,0:T(4,128)} %device_ref.3, s32[3,512]{1,0:T(4,128)} %cell_ref.1, s32[1,128]{1,0:T(1,128)} %slice.15.flags_ref, f32[81,10,2,128]{3,2,1,0:T(2,128)} %ensemble_ref.1), custom_call_target="tpu_custom_call" | custom-call | tf_op jit(solution)/shard_map/payload/pallas_call | solution.py:334
  5.3 0.7 slice_reduce_fusion
  6.0 0.3 broadcast_in_dim.2
  6.4 44.3 %all_to_all.8 = f32[256,1,640]{2,1,0:T(1,128)S(1)} all-to-all(f32[256,1,640]{2,1,0:T(1,128)S(1)} %broadcast_in_dim.2), channel_id=1, replica_groups=mesh['y'=8,'x'=4,'c'=2,'z'=8] {'y','x','z'}, dimensions={0} | all-to-all | bytes 1310720 | tf_op jit(solution)/shard_map/all_to_all | solution.py:357
  50.7 0.0 copy-start
  50.8 0.0 copy-start.1
  50.8 4.8 %collective-permute-start = (f32[256,640]{1,0:T(8,128)S(1)}, f32[256,640]{1,0:T(8,128)S(1)}, u32[]{:S(2)}, u32[]{:S(2)}) collective-permute-start(f32[256,640]{1,0:T(8,128)S(1)} %bitcast.17), channel_id=1, source_target_pairs={{0,8},{8,0},{1,9},{9,1},{2,10},{10,2},{3,11},{11,3},{4,12},{12,4},... | collective-permute-start | bytes 1966088 | tf_op jit(solution)/shard_map/ppermute | solution.py:358
  55.6 0.6 copy.21
  56.2 0.0 copy-done
  56.2 0.7 reshape.27
  56.9 0.0 copy-done.1
  56.9 0.5 dot_general.8
  57.4 3.0 %positions.1.info_ref = f32[512,128]{1,0:T(8,128)} custom-call(s32[1]{0:T(128)} %bitcast.1.core_ref, s32[3,512]{1,0:T(4,128)} %order_ref.1, s32[3,512]{1,0:T(4,128)} %device_ref.3, f32[3,512]{1,0:T(4,128)} %values_ref.1, f32[3,512]{1,0:T(4,128)} %errors_ref.1), custom_call_target="tpu_custom_call" | custom-call | tf_op jit(solution)/shard_map/positions/pallas_call | solution.py:253
  60.5 0.0 collective-permute-done.other_ref
  60.5 0.0 copy-start.2
  60.5 0.8 copy-done.2
  61.3 35.5 %filter.1 = f32[128,128]{1,0:T(8,128)} custom-call(f32[256,640]{1,0:T(8,128)} %bitcast.18, f32[256,640]{1,0:T(8,128)} %copy-done.2, f32[512,128]{1,0:T(8,128)} %positions.1.info_ref, s32[3,64]{1,0:T(4,128)} %bitcast.19), custom_call_target="tpu_custom_call" | custom-call | tf_op jit(solution)/shard_map/filter/pallas_call | solution.py:264
  96.8 1.3 %fusion = f32[81,10,2,128]{3,0,2,1:T(8,128)S(1)} fusion(f32[10,2,128,81]{2,1,0,3:T(2,128)S(1)} %dot_general.8, f32[128,128]{1,0:T(8,128)} %filter.1), kind=kOutput, calls=%fused_computation | convolution fusion | flops 100776960 | bytes 1703936 | tf_op jit(solution)/shard_map/dot_general | solution.py:361
  98.2 1.3 %copy.12 = f32[81,10,2,128]{3,2,1,0:T(2,128)} copy(f32[81,10,2,128]{3,0,2,1:T(8,128)S(1)} %fusion) | data formatting | bytes 1658880 | tf_op jit(solution)/shard_map/dot_general | solution.py:361
  (2 shorter events, 0.1 us)
Async XLA Ops:
  0.0 0.7 copy-start.3
  50.7 5.5 %copy-start = (f32[81,10,2,128]{3,2,1,0:T(2,128)S(1)}, f32[81,10,2,128]{3,2,1,0:T(2,128)}, u32[]{:S(2)}) copy-start(f32[81,10,2,128]{3,2,1,0:T(2,128)} %ensemble_ref.1) | copy-start | bytes 2488324
  50.8 6.1 %copy-start.1 = (f32[256,1,640]{2,0,1:T(8,128)}, f32[256,1,640]{2,0,1:T(8,128)S(1)}, u32[]{:S(2)}) copy-start(f32[256,1,640]{2,0,1:T(8,128)S(1)} %copy.20) | copy-start | bytes 1966084
  50.8 9.7 %collective-permute-start = (f32[256,640]{1,0:T(8,128)S(1)}, f32[256,640]{1,0:T(8,128)S(1)}, u32[]{:S(2)}, u32[]{:S(2)}) collective-permute-start(f32[256,640]{1,0:T(8,128)S(1)} %bitcast.17), channel_id=1, source_target_pairs={{0,8},{8,0},{1,9},{9,1},{2,10},{10,2},{3,11},{11,3},{4,12},{12,4},... | collective-permute-start | bytes 1966088 | tf_op jit(solution)/shard_map/ppermute | solution.py:358
  60.5 0.8 copy-start.2

commit v4 on v3

--- a/solution.py
+++ b/solution.py
@@ -78,7 +78,7 @@
 
 def main_kernel(own_ref, other_ref, info_ref, coupling_ref, out_ref,
                 buf_ref, z_ref, x_ref, r_ref, mask_ref, w_ref, vt_ref, wk_ref, vk_ref,
-                vx_ref, sx_ref, wst_ref, vv_ref, sh_ref, sl_ref, keep_ref):
+                vx_ref, sx_ref, sy_ref, wst_ref, vv_ref, sh_ref, sl_ref, keep_ref):
     lanes = iota((64, 128), 1)
     first = lanes == 0
     valid = lanes < AUG
@@ -121,10 +121,14 @@
     x_ref[:, 0:128] = jnp.where((iota((128, 128), 0) == iota((128, 128), 1))
                                     & (iota((128, 128), 0) < AUG), 1.0, 0.0)
 
-    i0 = iota((GR, 1024), 0)
-    i1 = iota((GR, 1024), 1)
-    ahead = (i0 >> 4) - (i1 >> 7)
-    keep_ref[...] = jnp.where((ahead > 0) | ((ahead == 0) & ((i0 & 15) >= 8) & ((i1 & 31) < 8)), 1.0, 0.0)
+    i0 = iota((GR, 512), 0)
+    i1 = iota((GR, 512), 1)
+    ahead = (i0 >> 5) - (i1 >> 7)
+    block = (i0 & 31) >> 3
+    at = i1 & 127
+    inside = ((block >= 1) & (at < 8)) | ((block >= 2) & (at < 24)) \
+        | ((block == 3) & ((at < 32) | ((at >= 48) & (at < 72))))
+    keep_ref[...] = jnp.where((ahead > 0) | ((ahead == 0) & inside), 1.0, 0.0)
     for t in range(NB):
         n = (1152, 640, 128)[t]
         zs = [z_ref[i * 64:(i + 1) * 64, :] for i in range(OB)]
@@ -178,15 +182,30 @@
         v_hi, v_lo = split(vk)
         v_hl = jnp.concatenate([v_hi, v_lo], axis=1)
         groups = [slice(g * GR, g * GR + GR) for g in range(NOBS // GR)]
-        bts = [dot_nt(v_hl[r], w_hh[r]) + dot_nt(v_hi[r], w_lo[r]) for r in groups]
+        straight = [dot_nt(v_hl[r], w_hh[r]) + dot_nt(v_hi[r], w_lo[r]) for r in groups]
         a0 = iota((GR, GR), 0)
         a1 = iota((GR, GR), 1)
         pairs = ((a0 >> 4) == (a1 >> 4)) & ((a0 & 15) < 8) & ((a1 & 15) >= 8)
-        v12s = []
-        for r, bt in zip(groups, bts):
-            b_hi, b_lo = split(jnp.where(pairs, bt, 0.0))
+        quad = ((a0 >> 5) == (a1 >> 5)) & ((a0 & 31) < 16)
+        third = quad & ((a1 & 31) >= 16) & ((a1 & 31) < 24)
+        fourth = quad & ((a1 & 31) >= 24)
+        v12s, x3s, x4s, x34s = [], [], [], []
+        for r, st in zip(groups, straight):
+            b_hi, b_lo = split(jnp.where(pairs, st, 0.0))
             v12s.append(dot_nn(jnp.concatenate([b_hi, b_hi], axis=1),
                                jnp.concatenate([v_hi[r], v_lo[r]], axis=0)) + dot_nn(b_lo, v_hi[r]))
+        for r, st, v12 in zip(groups, straight, v12s):
+            p_hi, p_lo = split(v12)
+            bent = dot_nt(jnp.concatenate([p_hi, p_lo], axis=1), w_hh[r]) + dot_nt(p_hi, w_lo[r])
+            left = jnp.concatenate([jnp.where(third, st, 0.0), jnp.where(third, bent, 0.0),
+                                    jnp.where(fourth, st, 0.0), jnp.where(fourth, bent, 0.0)], axis=0)
+            l_hi, l_lo = split(left)
+            l_hh = jnp.concatenate([l_hi, l_hi], axis=1)
+            x = dot_nn(l_hh, jnp.concatenate([v_hi[r], v_lo[r]], axis=0)) + dot_nn(l_lo, v_hi[r])
+            x3s.append((x[0:GR], x[GR:2 * GR]))
+            x4s.append((x[2 * GR:3 * GR], x[3 * GR:]))
+            x = dot_nn(l_hh[0:2 * GR], jnp.concatenate([p_hi, p_lo], axis=0)) + dot_nn(l_lo[0:2 * GR], p_hi)
+            x34s.append((x[0:GR], x[GR:]))
         for g in range(NOBS // GR - 1):
             r = groups[g]
             s_hi, s_lo = split(dot_nt(w_hh[r.stop:], v_hl[r]) + dot_nt(w_lo[r.stop:], v_hi[r]))
@@ -195,38 +214,51 @@
         zero8 = jnp.zeros((8, 128), F32)
         for g, r in enumerate(groups):
             vg, v12 = vk[r], v12s[g]
-            for q in range(GR // 16):
-                piece = jnp.concatenate([vg[16 * q:16 * q + 8], vg[16 * q + 8:16 * q + 16],
-                                         v12[16 * q:16 * q + 8], zero8], axis=0)
-                for rep in range(4):
-                    vx_ref[q * 128 + rep * 32:q * 128 + rep * 32 + 32, :] = piece
+            for q in range(GR // 32):
+                at = 32 * q
+                vx_ref[128 * q:128 * q + 16, :] = vg[at:at + 16]
+                vx_ref[128 * q + 16:128 * q + 24, :] = v12[at:at + 8]
+                vx_ref[128 * q + 24:128 * q + 40, :] = vg[at + 16:at + 32]
+                vx_ref[128 * q + 40:128 * q + 48, :] = v12[at + 16:at + 24]
+                for e, (flat, both) in enumerate((x3s[g], x4s[g], x34s[g])):
+                    to = 128 * q + 48 + 24 * e
+                    vx_ref[to:to + 16, :] = flat[at:at + 16]
+                    vx_ref[to + 16:to + 24, :] = both[at:at + 8]
+                vx_ref[128 * q + 120:128 * q + 128, :] = zero8
             e_hi, e_lo = split(vx_ref[...])
             sx = dot_nt(w_hh[r], jnp.concatenate([e_hi, e_lo], axis=1)) + dot_nt(w_lo[r], e_hi)
-            sx = sx * keep_ref[...]
-            s_hi = sx.astype(BF16).astype(F32)
-            sx_ref[r, :] = jnp.where((iota((GR, 1024), 1) & 127) < 64, s_hi, sx - s_hi).astype(BF16)
+            s_hi, s_lo = split(sx * keep_ref[...])
+            sx_ref[r, :] = s_hi
+            sy_ref[r, :] = s_lo
 
         chunks = [slice(c, min(c + 256, n)) for c in range(0, n, 256)]
         wide = [slice(c, min(c + WIDE, n)) for c in range(0, n, WIDE)]
         for g, rows in enumerate(groups):
             lo_row = g * GR
-            for q in range(GR // 16):
-                top = lo_row + 16 * q
+            for q in range(GR // 32):
+                top = lo_row + 32 * q
                 mrow = 64 * (t % 2) + top // 8
-                lhs = sx_ref[top:lo_row + GR, q * 128:q * 128 + 96]
+                s_hi = sx_ref[top:lo_row + GR, q * 128:q * 128 + 128]
+                s_hh = jnp.concatenate([s_hi, s_hi], axis=1)
+                s_lo = sy_ref[top:lo_row + GR, q * 128:q * 128 + 128]
                 for c in chunks:
-                    m1 = mask_ref[mrow:mrow + 1, c]
-                    m2 = mask_ref[mrow + 1:mrow + 2, c]
-                    r1 = r_ref[top:top + 8, c] * m1
-                    r2 = r_ref[top + 8:top + 16, c] * m2
-                    e = jnp.concatenate([r1, r2, r1 * m2, jnp.zeros_like(r1)], axis=0)
-                    e_hi, e_lo = split(e)
-                    u = dot_nn(lhs, jnp.concatenate([e_hi, e_lo, e_hi], axis=0))
-                    if q < GR // 16 - 1:
-                        r_ref[top + 16:lo_row + GR, c] = r_ref[top + 16:lo_row + GR, c] + u[16:]
-                    f_hi, f_lo = split(jnp.concatenate([r1, r2 + m2 * u[8:16]], axis=0))
-                    wst_ref[16 * q:16 * q + 16, c] = f_hi
-                    wst_ref[GR + 16 * q:GR + 16 * q + 16, c] = f_lo
+                    m1, m2, m3, m4 = [mask_ref[mrow + b:mrow + b + 1, c] for b in range(4)]
+                    r1, r2, r3, r4 = [r_ref[top + 8 * b:top + 8 * b + 8, c] for b in range(4)]
+                    r1 = r1 * m1
+                    head = jnp.concatenate([r1, r2 * m2, r1 * m2], axis=0)
+                    b3 = r3 * m3
+                    by3 = head * m3
+                    f = jnp.concatenate([head, b3, r4 * m4, b3 * m4, by3, head * m4, by3 * m4,
+                                         jnp.zeros_like(r1)], axis=0)
+                    f_hi, f_lo = split(f)
+                    u = dot_nn(s_hh, jnp.concatenate([f_hi, f_lo], axis=0)) + dot_nn(s_lo, f_hi)
+                    if q < GR // 32 - 1:
+                        r_ref[top + 32:lo_row + GR, c] = r_ref[top + 32:lo_row + GR, c] + u[32:]
+                    w = jnp.concatenate([r1, (r2 + u[8:16]) * m2, (r3 + u[16:24]) * m3,
+                                         (r4 + u[24:32]) * m4], axis=0)
+                    f_hi, f_lo = split(w)
+                    wst_ref[32 * q:32 * q + 32, c] = f_hi
+                    wst_ref[GR + 32 * q:GR + 32 * q + 32, c] = f_lo
             later = NOBS - lo_row - GR
             g_hi, g_lo = split(vv_ref[0:XR, rows])
             if later:
@@ -276,13 +308,14 @@
             pltpu.VMEM((NOBS, 128), F32),
             pltpu.VMEM((NOBS, 128), F32),
             pltpu.VMEM((NOBS, 128), F32),
-            pltpu.VMEM((1024, 128), F32),
-            pltpu.VMEM((NOBS, 1024), BF16),
+            pltpu.VMEM((512, 128), F32),
+            pltpu.VMEM((NOBS, NOBS), BF16),
+            pltpu.VMEM((NOBS, NOBS), BF16),
             pltpu.VMEM((2 * GR, 1152), BF16),
             pltpu.VMEM((128, NOBS), F32),
             pltpu.VMEM((NOBS, NOBS), BF16),
             pltpu.VMEM((NOBS, NOBS), BF16),
-            pltpu.VMEM((GR, 1024), F32),
+            pltpu.VMEM((GR, NOBS), F32),
         ],
         compiler_params=pltpu.CompilerParams(vmem_limit_bytes=VMEM_LIMIT),
         name="filter",

time: 99.9 us -> 97.9 us (0.980)
  Pallas kernels: 42.6 us -> 40.6 us
    pallas_call x1, Pallas kernels: 35.5 us -> 33.5 us  [main_call(): pl.pallas_call(main_kernel, out_shape=jax.ShapeDtypeStruct((128, 128), F3...]
where the time goes in v4:
time: 97.9 us; the launch traced here: 97.5 us
  blocking collectives  44.3 us (45%)
  Pallas kernels  40.6 us (41%)
  local copies, waits for them, and re-layouts  6.34 us (6%)
  starting transfers between devices  4.84 us (5%)
  matrix products  1.3 us (1%)
    all_to_all x1, blocking collectives, local(): lax.all_to_all(jnp.broadcast_to(payload[0:1], (group, PAY)), ('y', 'x', '...  44.3 us
    pallas_call x1, Pallas kernels, main_call(): pl.pallas_call(main_kernel, out_shape=jax.ShapeDtypeStruct((128, 128), F3...  33.5 us
    ppermute x1, starting transfers between devices, local(): other = lax.ppermute(own, 'c', [(0, 1), (1, 0)])  4.84 us
    pallas_call x1, Pallas kernels, payload_call(): pl.pallas_call(payload_kernel, out_shape=jax.ShapeDtypeStruct((8, PAY), F...  3.98 us
    pallas_call x1, Pallas kernels, index_call(): pl.pallas_call(index_kernel, out_shape=jax.ShapeDtypeStruct((NOBS, 128),...  3.04 us
    unnamed x10, local copies, waits for them, and re-layouts  2.14 us
  transfers between devices with their start and end apart: 1, of which 0 were waited for; matrix products, arithmetic and copies ran while one was open for 2% of the time, Pallas kernels for 3%

profile of v4, /device:TPU:1, one launch (start us, length us, event | category | flops | bytes accessed | tf_op | source)
XLA Modules:
  0.0 97.5 jit_solution(7433600610016008327)
XLA Ops:
  0.0 0.0 copy-start.3
  0.0 0.7 copy-done.3
  0.7 0.1 reshape.24
  0.8 0.5 slice.15.flags_ref
  1.3 4.0 %payload.1 = f32[8,640]{1,0:T(8,128)} custom-call(s32[1]{0:T(128)} %bitcast.me_ref, s32[3,512]{1,0:T(4,128)} %device_ref.3, s32[3,512]{1,0:T(4,128)} %cell_ref.1, s32[1,128]{1,0:T(1,128)} %slice.15.flags_ref, f32[81,10,2,128]{3,2,1,0:T(2,128)} %ensemble_ref.1), custom_call_target="tpu_custom_call" | custom-call | tf_op jit(solution)/shard_map/payload/pallas_call | solution.py:367
  5.3 0.7 slice_reduce_fusion
  6.0 0.3 broadcast_in_dim.2
  6.4 44.3 %all_to_all.8 = f32[256,1,640]{2,1,0:T(1,128)S(1)} all-to-all(f32[256,1,640]{2,1,0:T(1,128)S(1)} %broadcast_in_dim.2), channel_id=1, replica_groups=mesh['y'=8,'x'=4,'c'=2,'z'=8] {'y','x','z'}, dimensions={0} | all-to-all | bytes 1310720 | tf_op jit(solution)/shard_map/all_to_all | solution.py:390
  50.7 0.0 copy-start
  50.8 0.0 copy-start.1
  50.8 4.8 %collective-permute-start = (f32[256,640]{1,0:T(8,128)S(1)}, f32[256,640]{1,0:T(8,128)S(1)}, u32[]{:S(2)}, u32[]{:S(2)}) collective-permute-start(f32[256,640]{1,0:T(8,128)S(1)} %bitcast.17), channel_id=1, source_target_pairs={{0,8},{8,0},{1,9},{9,1},{2,10},{10,2},{3,11},{11,3},{4,12},{12,4},... | collective-permute-start | bytes 1966088 | tf_op jit(solution)/shard_map/ppermute | solution.py:391
  55.6 0.6 copy.21
  56.2 0.0 copy-done
  56.2 0.7 reshape.27
  56.9 0.0 copy-done.1
  56.9 0.5 dot_general.8
  57.4 3.0 %positions.1.info_ref = f32[512,128]{1,0:T(8,128)} custom-call(s32[1]{0:T(128)} %bitcast.1.core_ref, s32[3,512]{1,0:T(4,128)} %order_ref.1, s32[3,512]{1,0:T(4,128)} %device_ref.3, f32[3,512]{1,0:T(4,128)} %values_ref.1, f32[3,512]{1,0:T(4,128)} %errors_ref.1), custom_call_target="tpu_custom_call" | custom-call | tf_op jit(solution)/shard_map/positions/pallas_call | solution.py:285
  60.5 0.0 collective-permute-done.other_ref
  60.5 0.0 copy-start.2
  60.5 0.8 copy-done.2
  61.3 33.5 %filter.1 = f32[128,128]{1,0:T(8,128)} custom-call(f32[256,640]{1,0:T(8,128)} %bitcast.18, f32[256,640]{1,0:T(8,128)} %copy-done.2, f32[512,128]{1,0:T(8,128)} %positions.1.info_ref, s32[3,64]{1,0:T(4,128)} %bitcast.19), custom_call_target="tpu_custom_call" | custom-call | tf_op jit(solution)/shard_map/filter/pallas_call | solution.py:296
  94.8 1.3 %fusion = f32[81,10,2,128]{3,0,2,1:T(8,128)S(1)} fusion(f32[10,2,128,81]{2,1,0,3:T(2,128)S(1)} %dot_general.8, f32[128,128]{1,0:T(8,128)} %filter.1), kind=kOutput, calls=%fused_computation | convolution fusion | flops 100776960 | bytes 1703936 | tf_op jit(solution)/shard_map/dot_general | solution.py:394
  96.2 1.3 %copy.12 = f32[81,10,2,128]{3,2,1,0:T(2,128)} copy(f32[81,10,2,128]{3,0,2,1:T(8,128)S(1)} %fusion) | data formatting | bytes 1658880 | tf_op jit(solution)/shard_map/dot_general | solution.py:394
  (2 shorter events, 0.1 us)
Async XLA Ops:
  0.0 0.7 copy-start.3
  50.7 5.5 %copy-start = (f32[81,10,2,128]{3,2,1,0:T(2,128)S(1)}, f32[81,10,2,128]{3,2,1,0:T(2,128)}, u32[]{:S(2)}) copy-start(f32[81,10,2,128]{3,2,1,0:T(2,128)} %ensemble_ref.1) | copy-start | bytes 2488324
  50.8 6.1 %copy-start.1 = (f32[256,1,640]{2,0,1:T(8,128)}, f32[256,1,640]{2,0,1:T(8,128)S(1)}, u32[]{:S(2)}) copy-start(f32[256,1,640]{2,0,1:T(8,128)S(1)} %copy.20) | copy-start | bytes 1966084
  50.8 9.7 %collective-permute-start = (f32[256,640]{1,0:T(8,128)S(1)}, f32[256,640]{1,0:T(8,128)S(1)}, u32[]{:S(2)}, u32[]{:S(2)}) collective-permute-start(f32[256,640]{1,0:T(8,128)S(1)} %bitcast.17), channel_id=1, source_target_pairs={{0,8},{8,0},{1,9},{9,1},{2,10},{10,2},{3,11},{11,3},{4,12},{12,4},... | collective-permute-start | bytes 1966088 | tf_op jit(solution)/shard_map/ppermute | solution.py:391
  60.5 0.8 copy-start.2
